TPU v7x, 256 devices: a whole 4x4x8 slice. The times are simulated.
256 devices in a mesh: chan: 128 (over y, x, z), tm: 2 (over core).
Axes of the slice: x: 4, y: 4, z: 8, core: 2. Of those that a mesh axis runs over, the one named last changes fastest.
Arguments:
- voltages: bfloat16 [2, 384, 1, 256, 2, 1024], P('tm', 'chan'), may hold values from -6 to 6
- filter_taps: float32 [4, 256], replicated, may hold values from -4 to 4
- block_mask: int32 [36, 256], P(None, 'chan'), may hold values 0 or 1
Outputs:
- visibilities: float32 [36, 256, 2, 128, 128], P('tm', 'chan')
Inputs may be any that keep to these rules, and one draw needn't show every extreme that they name: `block_mask`: 1 marks a block pair that is correlated in that channel, 0 one that is not.
All inputs are finite; a program needn't handle non-finite values.
Results may differ from a plain program's by a relative error of at most 0.0044.
Values may be sent and summed in bfloat16 or wider, within the bound.
A program may use at most 128 MiB of HBM per device.

v0:
```python
import math

import jax
import jax.numpy as jnp
from jax import lax
from jax.sharding import PartitionSpec as P

FINE = 256
BLOCK_ST = 64
NBLK = 8
TAPS = 4


def from_behind(value, axis, steps):
    count = lax.axis_size(axis)
    first, last = (max(0, -steps), min(count, count - steps))
    return lax.ppermute(value, axis, [(source, source + steps) for source in range(first, last)])


def dft_table(size):
    index = jnp.arange(size, dtype=jnp.int32)
    product = index[:, None] * index[None, :] % size
    angle = product.astype(jnp.float32) * (2.0 * math.pi / size)
    cosine = jnp.cos(angle) / math.sqrt(size)
    sine = jnp.sin(angle) / math.sqrt(size)
    upper = jnp.stack([cosine, sine], 2)
    lower = jnp.stack([-sine, cosine], 2)
    return jnp.stack([upper, lower], 1).reshape(2 * size, 2 * size).astype(jnp.bfloat16)


def spectra_of(extended, filter_taps, table):
    count = extended.shape[0] - (TAPS - 1)
    weighted = jnp.zeros((count,) + extended.shape[1:], jnp.float32)
    for p in range(TAPS):
        piece = extended[TAPS - 1 - p : TAPS - 1 - p + count]
        weighted = weighted + filter_taps[p][None, None, :, None, None] * piece
    weighted = weighted.astype(jnp.bfloat16)
    shape = weighted.shape
    flat = weighted.reshape(shape[0], shape[1], 2 * shape[2], shape[4])
    result = jnp.einsum("kn,fgni->fgki", table, flat, preferred_element_type=jnp.float32)
    return result.astype(jnp.bfloat16).reshape(shape[0], shape[1] * shape[2], 2, shape[4])


def pair_block(ordered, mask_local, lower, upper, scale):
    width = 2 * BLOCK_ST
    channels = ordered.shape[0]
    weights = mask_local.astype(jnp.float32) * scale
    pieces = []
    base = 0
    for first in range(NBLK):
        row_len = NBLK - first
        begin = max(lower, base)
        finish = min(upper, base + row_len)
        second_lo = first + begin - base
        second_hi = first + finish - base
        left = ordered[:, :, first * width : (first + 1) * width]
        right = ordered[:, :, second_lo * width : second_hi * width]
        count = finish - begin

        def compute(left=left, right=right, count=count):
            combos = jnp.einsum("hcif,hdjf->hcdij", left, right, preferred_element_type=jnp.float32)
            real_sum = combos[:, 0, 0] + combos[:, 1, 1]
            imag_sum = combos[:, 1, 0] - combos[:, 0, 1]
            joined = jnp.stack([real_sum, imag_sum], 1)
            joined = joined.reshape(channels, 2, width, count, width)
            return jnp.transpose(joined, (3, 0, 1, 2, 4))

        pieces.append(compute())
        base = base + row_len
    stacked = jnp.concatenate(pieces, 0)
    return stacked * weights[:, :, None, None, None]


def per_device(voltages, filter_taps, block_mask):
    frames = voltages[0]
    before = from_behind(frames, "chan", 1)
    extended = jnp.concatenate([before, frames], 0)
    spectra = spectra_of(extended, filter_taps, dft_table(FINE))
    turned = lax.all_to_all(spectra, "chan", split_axis=1, concat_axis=0, tiled=True)
    subints = lax.axis_size("tm")
    scale = 1.0 / math.sqrt(turned.shape[0] * subints)
    ordered = jnp.transpose(turned, (1, 2, 3, 0))
    complete = pair_block(ordered, block_mask, 0, block_mask.shape[0], scale)
    return lax.psum_scatter(complete, "tm", scatter_dimension=0, tiled=True)


def solution(mesh):
    in_specs = (P("tm", "chan", None, None, None, None), P(), P(None, "chan"))
    out_specs = P("tm", "chan", None, None, None)
    return jax.shard_map(
        per_device, mesh=mesh, in_specs=in_specs, out_specs=out_specs, check_vma=False
    )
```

profile of v0, /device:TPU:65, one launch (start us, length us, event | category | flops | bytes accessed | tf_op | source)
XLA Modules:
  0.0 305.3 jit_solution(2030948430187339837)
XLA Ops:
  6.5 2.9 copy.157
  9.4 3.5 %collective-permute-start = (bf16[3,1,256,2,1024]{4,2,3,1,0:T(8,128)(2,1)S(1)}, bf16[3,1,256,2,1024]{4,2,3,1,0:T(8,128)(2,1)}, u32[]{:S(2)}, u32[]{:S(2)}) collective-permute-start(bf16[3,1,256,2,1024]{4,2,3,1,0:T(8,128)(2,1)S(1)} %bitcast.202), channel_id=1, source_target_pairs={{0,2},{2,4},{4,6},{6,8},{8,10},{10,12},{12,14},{14,16},{16,18},{18... | collective-permute-start | bytes 9437192 | tf_op jit(solution)/shard_map/ppermute | solution.py:17
  16.0 23.8 %copy.114 = bf16[256,2,256,2]{3,2,1,0:T(8,128)(2,1)} copy(bf16[256,2,256,2]{2,0,3,1:T(8,128)(2,1)} %pad_maximum_fusion.1) | data formatting | bytes 1048576 | tf_op jit(solution)/shard_map/stack | solution.py:28
  39.7 49.6 %reshape.470 = bf16[512,512,1]{1,0,2:T(8,128)(2,1)} reshape(bf16[256,2,256,2]{3,2,1,0:T(8,128)(2,1)} %copy.114) | data formatting | bytes 1048576 | tf_op jit(solution)/shard_map/convert_element_type | solution.py:28
  89.3 5.4 %add_convert_fusion = bf16[3,1,256,2,1024]{4,2,3,1,0:T(8,128)(2,1)S(1)} fusion(bf16[3,1,256,2,1024]{4,2,3,1,0:T(8,128)(2,1)} %collective-permute-done, bf16[3,1,256,2,1024]{4,2,3,1,0:T(8,128)(2,1)S(1)} %bitcast.203, f32[256]{0:T(256)S(1)} %bitcast.220, f32[256]{0:T(256)S(1)} %bitcast.221, f32[256]{0:T(256)S(1)} %bitcast.219, f32[256]{0:T(256)S(1)} %bitcast.218), kind=kLoop, calls=%fused_computation.2 | loop fusion | flops 22020096 | bytes 9441280 | tf_op jit(solution)/shard_map/convert_element_type | solution.py:37
  94.8 3.2 %copy.113 = bf16[3,1,256,2,1024]{4,3,2,0,1:T(2,128)(2,1)S(1)} copy(bf16[3,1,256,2,1024]{4,2,3,1,0:T(8,128)(2,1)S(1)} %add_convert_fusion) | data formatting | bytes 6291456 | tf_op jit(solution)/shard_map/convert_element_type | solution.py:37
  98.0 3.2 %reshape.468 = bf16[3,512,1024]{2,1,0:T(8,128)(2,1)} reshape(bf16[3,1,256,2,1024]{4,3,2,0,1:T(2,128)(2,1)S(1)} %copy.113) | data formatting | bytes 6291456 | tf_op jit(solution)/shard_map/reshape.4
  101.2 5.5 %convert_bitcast_fusion = bf16[3,1,512,1024]{3,2,0,1:T(8,128)(2,1)} fusion(bf16[512,512,1]{1,0,2:T(8,128)(2,1)} %reshape.470, bf16[3,512,1024]{2,1,0:T(8,128)(2,1)} %reshape.468), kind=kOutput, calls=%fused_computation.9 | convolution fusion | flops 1612185600 | bytes 6815744 | tf_op jit(solution)/shard_map/kn,fgni->fgki/dot_general | solution.py:40
  106.7 4.0 %reshape.469 = bf16[3,256,2,1024]{3,2,1,0:T(2,128)(2,1)S(1)} reshape(bf16[3,1,512,1024]{3,2,0,1:T(8,128)(2,1)} %convert_bitcast_fusion) | data formatting | bytes 6291456 | tf_op jit(solution)/shard_map/reshape | solution.py:41
  110.8 3.8 %copy.115 = bf16[3,256,2,1024]{3,2,0,1:T(2,128)(2,1)} copy(bf16[3,256,2,1024]{3,2,1,0:T(2,128)(2,1)S(1)} %reshape.469) | data formatting | bytes 6291456 | tf_op jit(solution)/shard_map/reshape | solution.py:41
  114.6 13.4 %all-to-all-start = ((bf16[3,256,2,1024]{3,2,0,1:T(2,128)(2,1)}), bf16[3,256,2,1024]{3,2,0,1:T(2,128)(2,1)S(1)}, u32[]{:S(2)}, u32[]{:S(2)}) async-start(bf16[3,256,2,1024]{3,2,0,1:T(2,128)(2,1)} %copy.115), calls=%async_computation | async-start | bytes 6291456 | tf_op jit(solution)/shard_map/all_to_all | solution.py:79
  128.8 71.7 %all-to-all-done = bf16[3,256,2,1024]{3,2,0,1:T(2,128)(2,1)S(1)} async-done(((bf16[3,256,2,1024]{3,2,0,1:T(2,128)(2,1)}), bf16[3,256,2,1024]{3,2,0,1:T(2,128)(2,1)S(1)}, u32[]{:S(2)}, u32[]{:S(2)}) %all-to-all-start) | async-done | bytes 3145760 | tf_op jit(solution)/shard_map/all_to_all | solution.py:79
  200.4 3.8 %copy.117 = bf16[128,3,2,2,1024]{4,3,2,1,0:T(2,128)(2,1)} copy(bf16[128,3,2,2,1024]{4,3,1,2,0:T(2,128)(2,1)S(1)} %bitcast.200) | data formatting | bytes 6291456 | tf_op jit(solution)/shard_map/all_to_all | solution.py:79
  204.2 7.3 %copy.118 = bf16[384,2,2,1024]{0,3,2,1:T(8,128)(2,1)S(1)} copy(bf16[384,2,2,1024]{3,2,1,0:T(2,128)(2,1)} %bitcast.201) | data formatting | bytes 6291456 | tf_op jit(solution)/shard_map/all_to_all | solution.py:79
  212.9 3.0 fusion.9
  215.8 2.6 fusion.11
  218.5 2.4 fusion.13
  230.8 3.4 %slice_add_fusion.1 = (f32[2,1,1,128,896]{3,4,1,2,0:T(8,128)}, f32[2,1,1,128,896]{3,4,1,2,0:T(8,128)}) fusion(f32[2,2,2,128,896]{3,4,1,2,0:T(8,128)} %fusion.9), kind=kLoop, calls=%fused_computation.39 | loop fusion | flops 458752 | bytes 5505024 | tf_op jit(solution)/shard_map/add | solution.py:62
  234.2 2.6 copy.122
  236.8 2.4 copy.121
  240.6 2.5 copy.124
  243.0 2.3 copy.123
  272.5 4.9 %broadcast_multiply_fusion = f32[36,2,2,128,128]{4,3,2,1,0:T(8,128)} fusion(f32[36,2,2,128,128]{4,3,2,1,0:T(8,128)S(1)} %constant_dynamic-update-slice_fusion, f32[36,2]{1,0:T(8,128)S(1)} %copy-done.18), kind=kLoop, calls=%fused_computation.3 | loop fusion | flops 2359296 | bytes 18874656 | tf_op jit(solution)/shard_map/mul | solution.py:71
  277.5 21.0 %reduce-scatter.2.cloned.1.call-done = f32[18,2,2,128,128]{4,3,2,1,0:T(8,128)} async-done(((f32[36,2,2,128,128]{4,3,2,1,0:T(8,128)}), f32[18,2,2,128,128]{4,3,2,1,0:T(8,128)}) %reduce-scatter.2.cloned.1.call-update) | async-done | bytes 4718608 | tf_op jit(solution)/shard_map/reduce_scatter | solution.py:84
  (85 shorter events, 43.4 us)
Async XLA Ops:
  9.4 79.9 %collective-permute-start = (bf16[3,1,256,2,1024]{4,2,3,1,0:T(8,128)(2,1)S(1)}, bf16[3,1,256,2,1024]{4,2,3,1,0:T(8,128)(2,1)}, u32[]{:S(2)}, u32[]{:S(2)}) collective-permute-start(bf16[3,1,256,2,1024]{4,2,3,1,0:T(8,128)(2,1)S(1)} %bitcast.202), channel_id=1, source_target_pairs={{0,2},{2,4},{4,6},{6,8},{8,10},{10,12},{12,14},{14,16},{16,18},{18... | collective-permute-start | bytes 9437192 | tf_op jit(solution)/shard_map/ppermute | solution.py:17
  39.7 49.6 %copy-start.19 = (f32[4,256]{1,0:T(4,128)S(1)}, f32[4,256]{1,0:T(4,128)}, u32[]{:S(2)}) copy-start(f32[4,256]{1,0:T(4,128)} %param.4) | copy-start | bytes 12292
  114.6 13.5 %copy-start.20 = (s32[36,2]{0,1:T(2,128)S(1)}, s32[36,2]{0,1:T(2,128)}, u32[]{:S(2)}) copy-start(s32[36,2]{0,1:T(2,128)} %param.5) | copy-start | bytes 868
  114.6 85.8 %all-to-all-start = ((bf16[3,256,2,1024]{3,2,0,1:T(2,128)(2,1)}), bf16[3,256,2,1024]{3,2,0,1:T(2,128)(2,1)S(1)}, u32[]{:S(2)}, u32[]{:S(2)}) async-start(bf16[3,256,2,1024]{3,2,0,1:T(2,128)(2,1)} %copy.115), calls=%async_computation | async-start | bytes 6291456 | tf_op jit(solution)/shard_map/all_to_all | solution.py:79
  128.0 170.5 %reduce-scatter.2.cloned.1.call-start = ((), (), s32[]{:S(2)}) async-start(), calls=%async_computation.2 | async-start | bytes 14155776 | tf_op jit(solution)/shard_map/reduce_scatter | solution.py:84
  234.2 5.0 %copy-start = (f32[2,2,2,128,768]{3,4,1,2,0:T(8,128)S(1)}, f32[2,2,2,128,768]{3,4,1,2,0:T(8,128)}, u32[]{:S(2)}) copy-start(f32[2,2,2,128,768]{3,4,1,2,0:T(8,128)} %fusion.11) | copy-start | bytes 9437188
  240.6 4.8 %copy-start.1 = (f32[2,2,2,128,640]{3,4,1,2,0:T(8,128)S(1)}, f32[2,2,2,128,640]{3,4,1,2,0:T(8,128)}, u32[]{:S(2)}) copy-start(f32[2,2,2,128,640]{3,4,1,2,0:T(8,128)} %fusion.13) | copy-start | bytes 7864324
  246.5 3.6 %copy-start.2 = (f32[2,2,2,128,512]{3,4,1,2,0:T(8,128)S(1)}, f32[2,2,2,128,512]{3,4,1,2,0:T(8,128)}, u32[]{:S(2)}) copy-start(f32[2,2,2,128,512]{3,4,1,2,0:T(8,128)} %convolution_bitcast_fusion) | copy-start | bytes 6291460
  251.3 4.2 %copy-start.3 = (f32[2,2,2,128,384]{3,4,1,2,0:T(8,128)S(1)}, f32[2,2,2,128,384]{3,4,1,2,0:T(8,128)}, u32[]{:S(2)}) copy-start(f32[2,2,2,128,384]{3,4,1,2,0:T(8,128)} %convolution_bitcast_fusion.1) | copy-start | bytes 4718596
  251.3 9.1 %copy-start.4 = (f32[2,2,2,128,256]{3,4,1,2,0:T(8,128)S(1)}, f32[2,2,2,128,256]{3,4,1,2,0:T(8,128)}, u32[]{:S(2)}) copy-start(f32[2,2,2,128,256]{3,4,1,2,0:T(8,128)} %convolution_bitcast_fusion.2) | copy-start | bytes 3145732
  256.5 11.9 %copy-start.5 = (f32[2,1,128,8,128]{4,2,1,0,3:T(8,128)S(1)}, f32[2,1,128,8,128]{4,2,1,0,3:T(8,128)}, u32[]{:S(2)}) copy-start(f32[2,1,128,8,128]{4,2,1,0,3:T(8,128)} %copy.120) | copy-start | bytes 3145732
  261.2 8.7 %copy-start.6 = (f32[2,1,128,7,128]{4,2,1,0,3:T(8,128)S(1)}, f32[2,1,128,7,128]{4,2,1,0,3:T(8,128)}, u32[]{:S(2)}) copy-start(f32[2,1,128,7,128]{4,2,1,0,3:T(8,128)} %copy.122) | copy-start | bytes 2752516
  261.2 8.7 %copy-start.7 = (f32[2,1,128,7,128]{4,2,1,0,3:T(8,128)S(1)}, f32[2,1,128,7,128]{4,2,1,0,3:T(8,128)}, u32[]{:S(2)}) copy-start(f32[2,1,128,7,128]{4,2,1,0,3:T(8,128)} %copy.121) | copy-start | bytes 2752516
  268.4 1.7 copy-start.8
  268.4 1.7 copy-start.9
  270.0 1.1 copy-start.10
  270.1 1.1 copy-start.11
  270.1 1.3 copy-start.12
  271.1 1.1 copy-start.13
  271.1 1.2 copy-start.14
  271.1 1.3 copy-start.16
  271.1 1.3 copy-start.17
  271.1 1.4 copy-start.15
  271.4 1.1 copy-start.18
Sparse Core Ops, SparseCore 0:
  277.6 20.8 reduce-scatter.1
where the time goes:
time: 309 us; the launch traced here: 305 us
  local copies, waits for them, and re-layouts  134 us (43%)
  waiting for transfers between devices  92.7 us (30%)
  other arithmetic  27.5 us (9%)
  matrix products  20.5 us (7%)
  starting transfers between devices  17 us (6%)
  between operations  13.7 us (4%)
    all_to_all x1, waiting for transfers between devices, per_device(): lax.all_to_all(spectra, 'chan', split_axis=1, concat_axis=0, tiled=True)  71.7 us
    convert_element_type x1, local copies, waits for them, and re-layouts, dft_table(): jnp.stack([upper, lower], 1).reshape(2 * size, 2 * size)  49.6 us
    another operation x1, local copies, waits for them, and re-layouts, dft_table(): jnp.stack([upper, lower], 1).reshape(2 * size, 2 * size)  23.8 us
    reduce_scatter x1, waiting for transfers between devices, per_device(): return lax.psum_scatter(complete, 'tm', scatter_dimension=0, tiled=True)  21 us
    dot_general x8, matrix products, compute(): jnp.einsum('hcif,hdjf->hcdij', left, right, preferred_element_type=jnp.fl...  15 us
    add x7, local copies, waits for them, and re-layouts, compute(): real_sum = combos[:, 0, 0] + combos[:, 1, 1]  14 us
    sub x7, local copies, waits for them, and re-layouts, compute(): imag_sum = combos[:, 1, 0] - combos[:, 0, 1]  13.9 us
    all_to_all x1, starting transfers between devices, per_device(): lax.all_to_all(spectra, 'chan', split_axis=1, concat_axis=0, tiled=True)  13.4 us
  transfers between devices with their start and end apart: 3, of which 2 were waited for; matrix products, arithmetic and copies ran while one was open for 25% of the time, Pallas kernels for 0%

commit v1 on v0

v1 whole, which is shorter than its diff:
```python
import functools
import math

import jax
import jax.numpy as jnp
import numpy as np
from jax import lax
from jax.experimental import pallas as pl
from jax.experimental.pallas import tpu as pltpu
from jax.sharding import PartitionSpec as P

TAPS = 4
FRAMES = 3
TILE = 128
NBLK = 8
STEPS = 4
MESH = pl.DeviceIdType.MESH
BF16 = jnp.bfloat16
F32 = jnp.float32

PAIRS = [(a, b) for a in range(NBLK) for b in range(a, NBLK)]


def dft_table(size):
    index = np.arange(size)
    angle = (index[:, None] * index[None, :] % size).astype(np.float32) * np.float32(2.0 * math.pi / size)
    cosine = np.cos(angle) / np.float32(math.sqrt(size))
    sine = np.sin(angle) / np.float32(math.sqrt(size))
    upper = np.stack([cosine, sine], 2)
    lower = np.stack([-sine, cosine], 2)
    table = np.stack([upper, lower], 1).reshape(size // 2, 2, 2, 2 * size)
    table = np.transpose(table, (1, 0, 2, 3)).reshape(2, size, 2 * size)
    return jnp.asarray(table.astype(BF16))


def turn_table(size):
    turn = np.zeros((size, size), np.float32)
    even = np.arange(0, size, 2)
    turn[even + 1, even] = 1.0
    turn[even, even + 1] = -1.0
    return jnp.asarray(turn.astype(BF16))


def pairs_ready(step, half):
    fresh = (step, step + STEPS)
    ready = []
    for a, b in PAIRS[half * 18 : half * 18 + 18]:
        if a % STEPS <= step and b % STEPS <= step and (a in fresh or b in fresh):
            ready.append((a, b))
    return ready


def digits(values):
    total = 0
    for place, value in enumerate(values):
        total += value * 8**place
    return total


def merged(ref):
    shape = ref.shape
    return ref.reshape(shape[:-3] + (shape[-3] * shape[-2], shape[-1]))


def kernel(
    count,
    v_ref, taps_ref, table_ref, turn_ref, weight_ref, out_ref,
    own, before, after, weighted, send, recv, other, left,
    load_sem, near_send, near_recv, send_sem, recv_sem, core_send, core_recv,
):
    me = lax.axis_index("chan")
    core = lax.axis_index("tm")
    fine = 2 * count
    rows = 2 * fine
    depth = 2 * FRAMES * count
    half = lax.rem(me, 2)
    up = lax.rem(me + 1, count)
    down = lax.rem(me + count - 1, count)

    own_rows, before_rows, after_rows = merged(own), merged(before), merged(after)
    send_rows, recv_rows, other_rows = merged(send), merged(recv), merged(other)

    def load(block):
        lanes = pl.ds(pl.multiple_of(block * TILE, TILE), TILE)
        return pltpu.make_async_copy(v_ref.at[:, :, :, lanes], own.at[block], load_sem.at[block])

    for step in range(STEPS):
        load((1 - half) * STEPS + step).start()
    for step in range(STEPS):
        load(half * STEPS + step).start()

    barrier = pltpu.get_barrier_semaphore()

    def greet(offset, carry):
        peer = lax.rem(me + offset, count)
        pl.semaphore_signal(barrier, inc=1, device_id={"chan": peer}, device_id_type=MESH)
        return carry

    lax.fori_loop(1, count, greet, 0)
    pl.semaphore_signal(barrier, inc=1, device_id={"tm": 1 - core}, device_id_type=MESH)
    pl.semaphore_wait(barrier, count)

    def near(step):
        block = (1 - half) * STEPS + step
        forward = pltpu.make_async_remote_copy(
            own.at[block], before.at[step], near_send.at[step, 0], near_recv.at[step, 0],
            device_id={"chan": up}, device_id_type=MESH,
        )
        backward = pltpu.make_async_remote_copy(
            own.at[block], after.at[step], near_send.at[step, 1], near_recv.at[step, 1],
            device_id={"chan": down}, device_id_type=MESH,
        )
        return forward, backward

    for step in range(STEPS):
        load((1 - half) * STEPS + step).wait()
        forward, backward = near(step)
        forward.start()
        backward.start()

    keep_before = jnp.where(me == 0, 0.0, 1.0).astype(F32)
    keep_own = jnp.where(me == count - 1, 0.0, 1.0).astype(F32)
    group = 16

    def across(step):
        return pltpu.make_async_remote_copy(
            recv.at[step], other.at[step], core_send.at[step], core_recv.at[step],
            device_id={"tm": 1 - core}, device_id_type=MESH,
        )

    for step in range(STEPS):
        block = half * STEPS + step
        load(block).wait()
        for copy in near(step):
            copy.wait_recv()

        def filter_rows(index, carry):
            at = pl.ds(pl.multiple_of(index * group, group), group)
            series = [before_rows[step, f, at, :].astype(F32) for f in range(FRAMES)]
            series += [own_rows[block, f, at, :].astype(F32) for f in range(FRAMES)]
            series += [after_rows[step, f, at, :].astype(F32) for f in range(FRAMES)]
            taps = [taps_ref[p, at, :] for p in range(TAPS)]
            for f in range(2 * FRAMES):
                inside = f % FRAMES
                total = taps[0] * series[FRAMES + f]
                for p in range(1, inside + 1):
                    total = total + taps[p] * series[FRAMES + f - p]
                past = taps[inside + 1] * series[FRAMES + f - inside - 1]
                for p in range(inside + 2, TAPS):
                    past = past + taps[p] * series[FRAMES + f - p]
                total = total + past * (keep_before if f < FRAMES else keep_own)
                weighted[at, f * TILE : (f + 1) * TILE] = total.astype(BF16)
            return carry

        lax.fori_loop(0, rows // group, filter_rows, 0)

        for parity in range(2):
            for pair in range(FRAMES):
                part = jnp.dot(
                    table_ref[parity], weighted[:, pair * 2 * TILE : (pair + 1) * 2 * TILE],
                    preferred_element_type=F32,
                ).astype(BF16)
                send_rows[step, parity, 2 * pair] = part[:, :TILE]
                send_rows[step, parity, 2 * pair + 1] = part[:, TILE:]

        @pl.when(me < count - 1)
        def _():
            place = pl.ds(3 * me, 2 * FRAMES)
            pltpu.make_async_copy(
                send.at[step, :, :, me], recv.at[step, half, :, place], recv_sem.at[step]
            ).start()

            def turn(offset, carry):
                peer = lax.rem(me + offset, count)
                pltpu.make_async_remote_copy(
                    send.at[step, :, :, peer], recv.at[step, half, :, place],
                    send_sem.at[step], recv_sem.at[step],
                    device_id={"chan": peer}, device_id_type=MESH,
                ).start()
                return carry

            lax.fori_loop(1, count, turn, 0)

        @pl.when(me == count - 1)
        def _():
            for first, place in ((0, FRAMES * count - FRAMES), (FRAMES, 0)):
                source = pl.ds(first, FRAMES)
                target = pl.ds(place, FRAMES)
                pltpu.make_async_copy(
                    send.at[step, :, source, count - 1], recv.at[step, 1, :, target], recv_sem.at[step]
                ).start()

                def turn(peer, carry):
                    pltpu.make_async_remote_copy(
                        send.at[step, :, source, peer], recv.at[step, 1, :, target],
                        send_sem.at[step], recv_sem.at[step],
                        device_id={"chan": peer}, device_id_type=MESH,
                    ).start()
                    return carry

                lax.fori_loop(0, count - 1, turn, 0)

    span = min(256, depth)

    def turn_block(step, side, source, base):
        block = side * STEPS + step

        def one(index, carry):
            parity = index // (depth // span)
            piece = lax.rem(index, depth // span)
            at = pl.ds(pl.multiple_of(piece * span, span), span)
            to = pl.ds(pl.multiple_of(base + piece * span, span), span)
            flat = source[step, side, parity, at, :].T
            left[block, parity, 0:TILE, to] = flat
            left[block, parity, TILE : 2 * TILE, to] = jnp.dot(
                flat, turn_ref[...], preferred_element_type=F32
            ).astype(BF16)
            return carry

        lax.fori_loop(0, 2 * (depth // span), one, 0)

    def turn_blocks(step, source, base):
        for side in range(2):
            block = side * STEPS + step
            if block == 2:
                turn_block(step, side, source, base)
            else:
                @pl.when(core == (0 if block < 2 else 1))
                def _():
                    turn_block(step, side, source, base)

    for step in range(STEPS):
        pltpu.make_async_copy(recv.at[step], recv.at[step], recv_sem.at[step]).wait()
        across(step).start()
        turn_blocks(step, recv_rows, 0)
        across(step).wait_recv()
        turn_blocks(step, other_rows, depth)

        lists = [pairs_ready(step, 0), pairs_ready(step, 1)]
        firsts = [digits([a for a, _ in pairs]) for pairs in lists]
        seconds = [digits([b for _, b in pairs]) for pairs in lists]

        def one_pair(index, carry):
            first_code, second_code = carry
            a = lax.rem(first_code, 8)
            b = lax.rem(second_code, 8)
            slot = a * NBLK - a * (a - 1) // 2 + b - a
            b_step = lax.rem(b, STEPS)
            b_side = b // STEPS
            for parity in range(2):
                sums = jnp.dot(
                    left[a, parity, :, 0:depth], recv_rows[b_step, b_side, parity],
                    preferred_element_type=F32,
                ) + jnp.dot(
                    left[a, parity, :, depth : 2 * depth], other_rows[b_step, b_side, parity],
                    preferred_element_type=F32,
                )
                sums = sums * weight_ref[slot, parity]
                out_ref[slot - 18 * core, parity, 0] = sums[:TILE]
                out_ref[slot - 18 * core, parity, 1] = sums[TILE:]
            return first_code // 8, second_code // 8

        total = len(lists[0]) + core * (len(lists[1]) - len(lists[0]))
        lax.fori_loop(
            0, total, one_pair,
            (firsts[0] + core * (firsts[1] - firsts[0]), seconds[0] + core * (seconds[1] - seconds[0])),
        )

    for step in range(STEPS):
        sent = send.at[step, :, :, pl.ds(0, count - 1)]
        pltpu.make_async_copy(sent, sent, send_sem.at[step]).wait()
        for copy in near(step):
            copy.wait_send()
        across(step).wait_send()


def per_device(count, voltages, filter_taps, block_mask):
    fine = 2 * count
    frames = voltages.reshape(FRAMES, fine, 2, NBLK * TILE)
    taps = jnp.broadcast_to(jnp.repeat(filter_taps, 2, 1)[:, :, None], (TAPS, 2 * fine, TILE))
    weights = block_mask.astype(F32) * F32(1.0 / math.sqrt(FRAMES * count * 2))
    depth = 2 * FRAMES * count
    dma = pltpu.SemaphoreType.DMA
    vmem = pl.BlockSpec(memory_space=pltpu.VMEM)
    return pl.pallas_call(
        functools.partial(kernel, count),
        out_shape=jax.ShapeDtypeStruct((18, 2, 2, TILE, TILE), F32),
        in_specs=[
            pl.BlockSpec(memory_space=pl.ANY), vmem, vmem, vmem,
            pl.BlockSpec(memory_space=pltpu.SMEM),
        ],
        out_specs=vmem,
        scratch_shapes=[
            pltpu.VMEM((NBLK, FRAMES, fine, 2, TILE), BF16),
            pltpu.VMEM((STEPS, FRAMES, fine, 2, TILE), BF16),
            pltpu.VMEM((STEPS, FRAMES, fine, 2, TILE), BF16),
            pltpu.VMEM((2 * fine, 2 * FRAMES * TILE), BF16),
            pltpu.VMEM((STEPS, 2, 2 * FRAMES, count, 2, TILE), BF16),
            pltpu.VMEM((STEPS, 2, 2, FRAMES * count, 2, TILE), BF16),
            pltpu.VMEM((STEPS, 2, 2, FRAMES * count, 2, TILE), BF16),
            pltpu.VMEM((NBLK, 2, 2 * TILE, 2 * depth), BF16),
            dma((NBLK,)), dma((STEPS, 2)), dma((STEPS, 2)), dma((STEPS,)), dma((STEPS,)),
            dma((STEPS,)), dma((STEPS,)),
        ],
        compiler_params=pltpu.CompilerParams(
            collective_id=0, has_side_effects=True, vmem_limit_bytes=50 * 2**20
        ),
        cost_estimate=pl.CostEstimate(flops=6 * 10**9, bytes_accessed=10**7, transcendentals=0),
        name="correlate",
    )(frames, taps, dft_table(fine), turn_table(min(256, depth)), weights)


def solution(mesh):
    in_specs = (P("tm", "chan", None, None, None, None), P(), P(None, "chan"))
    out_specs = P("tm", "chan", None, None, None)
    return jax.shard_map(
        functools.partial(per_device, mesh.shape["chan"]),
        mesh=mesh, in_specs=in_specs, out_specs=out_specs, check_vma=False,
    )
```

time: 309 us -> 142 us (0.46)
  Pallas kernels: 0 us -> 131 us
  local copies, waits for them, and re-layouts: 134 us -> 8.49 us
  waiting for transfers between devices: 92.7 us -> 0 us
  other arithmetic: 27.5 us -> 0.69 us
  matrix products: 20.5 us -> 0 us
  starting transfers between devices: 17 us -> 0 us
  between operations: 13.7 us -> 0.04 us
    pallas_call x0 -> x1, Pallas kernels: none -> 131 us  [per_device(): pl.pallas_call(functools.partial(kernel, count), out_shape=jax.ShapeDtype...]
    all_to_all x1 -> x0, waiting for transfers between devices: 71.7 us -> none  [per_device(): lax.all_to_all(spectra, 'chan', split_axis=1, concat_axis=0, tiled=True)]
    convert_element_type x2 -> x1, local copies, waits for them, and re-layouts: 52.8 us -> 0.1 us  [per_device(): weights = block_mask.astype(F32) * F32(1.0 / math.sqrt(FRAMES * count * 2))]
    another operation x3 -> x0, local copies, waits for them, and re-layouts: 28.8 us -> none  [the longest x1 23.8 us: dft_table(): jnp.stack([upper, lower], 1).reshape(2 * size, 2 * size)]
    reduce_scatter x1 -> x0, waiting for transfers between devices: 21 us -> none  [per_device(): return lax.psum_scatter(complete, 'tm', scatter_dimension=0, tiled=True)]
    dot_general x9 -> x0, matrix products: 20.5 us -> none  [the longest x8 15 us: compute(): jnp.einsum('hcif,hdjf->hcdij', left, right, preferred_element_type=jnp.fl...]
    add x7 -> x0, local copies, waits for them, and re-layouts: 14 us -> none  [compute(): real_sum = combos[:, 0, 0] + combos[:, 1, 1]]
    sub x7 -> x0, local copies, waits for them, and re-layouts: 13.9 us -> none  [compute(): imag_sum = combos[:, 1, 0] - combos[:, 0, 1]]
  transfers between devices with their start and end apart: 3 -> 0, of which waited for: 2 -> 0; matrix products, arithmetic and copies ran while one was open for 25% -> 0% of each run, Pallas kernels for 0% -> 0%
where the time goes in v1:
time: 142 us; the launch traced here: 140 us
  Pallas kernels  131 us (92%)
  local copies, waits for them, and re-layouts  8.49 us (6%)
    pallas_call x1, Pallas kernels, per_device(): pl.pallas_call(functools.partial(kernel, count), out_shape=jax.ShapeDtype...  131 us
    unnamed x6, local copies, waits for them, and re-layouts  7.85 us

profile of v1, /device:TPU:65, one launch (start us, length us, event | category | flops | bytes accessed | tf_op | source)
XLA Modules:
  0.0 139.8 jit_solution(12923275497647535766)
XLA Ops:
  0.0 0.7 convert_element_type.3
  0.7 0.1 copy.12
  0.8 0.8 copy.10
  1.6 0.1 broadcast_in_dim.10
  1.7 0.1 copy.11
  1.8 0.3 broadcast_in_dim.12.taps_ref
  2.2 0.0 copy-start
  2.2 1.0 copy-done
  3.2 0.0 copy-start.1
  3.2 0.9 copy-done.1
  4.1 130.6 %correlate.1 = f32[18,2,2,128,128]{4,3,2,1,0:T(8,128)} custom-call(bf16[3,256,2,1024]{3,2,1,0:T(2,128)(2,1)} %bitcast.3, f32[4,512,128]{2,1,0:T(8,128)S(1)} %broadcast_in_dim.12.taps_ref, bf16[2,256,512]{2,1,0:T(8,128)(2,1)S(1)} %copy-done, bf16[256,256]{1,0:T(8,128)(2,1)S(1)} %copy-done.1, f32[36,2]{1,0:T(8,128)S(1)} %broadcast_multiply_fusion.weight_ref), custom_call_target="tpu_custom_call" | custom-call | flops 6000000000 | bytes 10000000 | tf_op jit(solution)/shard_map/correlate/pallas_call | solution.py:285
  134.7 5.1 %copy.15 = f32[18,2,2,128,128]{4,3,2,1,0:T(8,128)} copy(f32[18,2,2,128,128]{4,3,2,1,0:T(8,128)} %correlate.1) | data formatting | bytes 9437184
  (1 shorter events, 0.0 us)
Async XLA Ops:
  2.2 1.0 copy-start
  3.2 0.9 copy-start.1

commit v2 on v1

v2 whole, which is shorter than its diff:
```python
import functools
import math

import jax
import jax.numpy as jnp
import numpy as np
from jax import lax
from jax.experimental import pallas as pl
from jax.experimental.pallas import tpu as pltpu
from jax.sharding import PartitionSpec as P

TAPS = 4
FRAMES = 3
TILE = 128
NBLK = 8
STEPS = 4
MESH = pl.DeviceIdType.MESH
BF16 = jnp.bfloat16
F32 = jnp.float32

PAIRS = [(a, b) for a in range(NBLK) for b in range(a, NBLK)]


def in_tiles(table):
    width = min(TILE, table.shape[-1])
    table = table.reshape(table.shape[:-2] + (table.shape[-2] // 2, 2, table.shape[-1] // width, width))
    return jnp.asarray(np.moveaxis(table, -2, -4).astype(BF16))


def whole(ref, *index):
    flat = merged(ref)
    return jnp.concatenate([flat[index + (tile,)] for tile in range(flat.shape[len(index)])], 1)


def dft_table(size):
    index = np.arange(size)
    angle = (index[:, None] * index[None, :] % size).astype(np.float32) * np.float32(2.0 * math.pi / size)
    cosine = np.cos(angle) / np.float32(math.sqrt(size))
    sine = np.sin(angle) / np.float32(math.sqrt(size))
    upper = np.stack([cosine, sine], 2)
    lower = np.stack([-sine, cosine], 2)
    table = np.stack([upper, lower], 1).reshape(size // 2, 2, 2, 2 * size)
    table = np.transpose(table, (1, 0, 2, 3)).reshape(2, size, 2 * size)
    return in_tiles(table)


def turn_table(size):
    turn = np.zeros((size, size), np.float32)
    even = np.arange(0, size, 2)
    turn[even + 1, even] = 1.0
    turn[even, even + 1] = -1.0
    return in_tiles(turn)


BLOCKS = ((0, 1, 3, 2), (5, 6, 7, 4))
PARTS = ((0, 1, 0, 2), (1, 2, 0, 2), (3, 1, 0, 1), (3, 1, 1, 1))


def place_of(block):
    half = block // STEPS
    return half * STEPS + BLOCKS[half].index(block)


def units_of(part, core):
    first, positions = PARTS[part][:2]
    ready = range(first + positions)
    fresh = range(first, first + positions)
    units = []
    for a in range(NBLK):
        row = []
        for b in range(a, NBLK):
            slot = PAIRS.index((a, b)) - 18 * core
            at = (place_of(a) % STEPS, place_of(b) % STEPS)
            if 0 <= slot < 18 and max(at) in fresh and max(at) in ready:
                row.append((b, slot))
        if len(row) % 2:
            row.append(row[-1])
        for (b, slot), (c, other) in zip(row[::2], row[1::2]):
            units.append((place_of(a), place_of(b), place_of(c), slot, other))
    return units


def codes_of(part):
    units = [units_of(part, core) for core in range(2)]
    count = max(len(units[0]), len(units[1]))
    codes = []
    for mine in units:
        while len(mine) < count:
            index = next(i for i, unit in enumerate(mine) if unit[3] != unit[4])
            a, b, c, slot, other = mine[index]
            mine[index : index + 1] = [(a, b, b, slot, slot), (a, c, c, other, other)]
        codes.append([
            sum(unit[field] * base**place for place, unit in enumerate(mine))
            for field, base in enumerate((8, 8, 8, 32, 32))
        ])
    return count, codes


def merged(ref):
    shape = ref.shape
    return ref.reshape(shape[:-3] + (shape[-3] * shape[-2], shape[-1]))


def kernel(
    count,
    v_ref, taps_ref, table_hbm, turn_hbm, mask_ref, out_ref,
    own, before, after, taps_wide, table_ref, turn_ref, weighted, send, recv, other, left,
    load_sem, const_sem, near_send, near_recv, send_sem, recv_sem, core_send, core_recv,
):
    me = lax.axis_index("chan")
    core = lax.axis_index("tm")
    fine = 2 * count
    rows = 2 * fine
    depth = 2 * FRAMES * count
    half = lax.rem(me, 2)
    up = lax.rem(me + 1, count)
    down = lax.rem(me + count - 1, count)
    scale = 1.0 / math.sqrt(FRAMES * count * 2)

    own_rows, before_rows, after_rows = merged(own), merged(before), merged(after)
    send_rows, recv_rows, other_rows = merged(send), merged(recv), merged(other)

    def place(away, position):
        side = 1 - half if away else half
        return side * STEPS + position

    def load(away, position):
        index = place(away, position)
        side = 1 - half if away else half
        block = BLOCKS[0][position] + side * (BLOCKS[1][position] - BLOCKS[0][position])
        lanes = pl.ds(pl.multiple_of(block * TILE, TILE), TILE)
        return pltpu.make_async_copy(v_ref.at[:, :, :, lanes], own.at[index], load_sem.at[index])

    constants = (
        pltpu.make_async_copy(table_hbm, table_ref, const_sem.at[0]),
        pltpu.make_async_copy(turn_hbm, turn_ref, const_sem.at[1]),
    )
    for away in (True, False):
        for position in range(STEPS):
            load(away, position).start()
    for copy in constants:
        copy.start()

    barrier = pltpu.get_barrier_semaphore()

    def greet(offset, carry):
        peer = lax.rem(me + offset, count)
        pl.semaphore_signal(barrier, inc=1, device_id={"chan": peer}, device_id_type=MESH)
        return carry

    lax.fori_loop(1, count, greet, 0)
    pl.semaphore_signal(barrier, inc=1, device_id={"tm": 1 - core}, device_id_type=MESH)

    row = lax.broadcasted_iota(jnp.int32, (rows, fine), 0)
    column = lax.broadcasted_iota(jnp.int32, (rows, fine), 1)
    spread = (row // 2 == column).astype(F32)
    for p in range(TAPS):
        wide = jnp.broadcast_to(taps_ref[p : p + 1, :], (TILE, fine))
        taps_wide[p] = lax.dot_general(
            spread, wide, (((1,), (1,)), ((), ())),
            precision=lax.Precision.HIGHEST, preferred_element_type=F32,
        )

    pl.semaphore_wait(barrier, count)

    def near(position):
        source = own.at[place(True, position)]
        return [
            pltpu.make_async_remote_copy(
                source, target.at[position], near_send.at[position, way], near_recv.at[position, way],
                device_id={"chan": peer}, device_id_type=MESH,
            )
            for way, (target, peer) in enumerate(((before, up), (after, down)))
        ]

    for position in range(STEPS):
        load(True, position).wait()
        for copy in near(position):
            copy.start()

    keep_before = jnp.where(me == 0, 0.0, 1.0).astype(F32)
    keep_own = jnp.where(me == count - 1, 0.0, 1.0).astype(F32)
    group = 16

    def filter_position(position):
        index = place(False, position)

        def filter_rows(step, carry):
            at = pl.ds(pl.multiple_of(step * group, group), group)
            series = [before_rows[position, f, at, :].astype(F32) for f in range(FRAMES)]
            series += [own_rows[index, f, at, :].astype(F32) for f in range(FRAMES)]
            series += [after_rows[position, f, at, :].astype(F32) for f in range(FRAMES)]
            taps = [taps_wide[p, at, :] for p in range(TAPS)]
            for f in range(2 * FRAMES):
                inside = f % FRAMES
                total = taps[0] * series[FRAMES + f]
                for p in range(1, inside + 1):
                    total = total + taps[p] * series[FRAMES + f - p]
                past = taps[inside + 1] * series[FRAMES + f - inside - 1]
                for p in range(inside + 2, TAPS):
                    past = past + taps[p] * series[FRAMES + f - p]
                total = total + past * (keep_before if f < FRAMES else keep_own)
                weighted[at, f * TILE : (f + 1) * TILE] = total.astype(BF16)
            return carry

        lax.fori_loop(0, rows // group, filter_rows, 0)

    def transform(position, parity):
        table = whole(table_ref, parity)
        for pair in range(FRAMES):
            part = jnp.dot(
                table, weighted[:, pair * 2 * TILE : (pair + 1) * 2 * TILE],
                preferred_element_type=F32,
            ).astype(BF16)
            send_rows[position, parity, 2 * pair] = part[:, :TILE]
            send_rows[position, parity, 2 * pair + 1] = part[:, TILE:]

    def extent(part):
        first, positions, channel, channels = PARTS[part]
        return pl.ds(first, positions), pl.ds(channel, channels)

    def send_part(part):
        at, channels = extent(part)

        def deliver(source_frames, side, frames):
            target = recv.at[at, side, channels, frames]
            pltpu.make_async_copy(
                send.at[at, channels, source_frames, me], target, recv_sem.at[part]
            ).start()

            def turn(offset, carry):
                peer = lax.rem(me + offset, count)
                pltpu.make_async_remote_copy(
                    send.at[at, channels, source_frames, peer], target,
                    send_sem.at[part], recv_sem.at[part],
                    device_id={"chan": peer}, device_id_type=MESH,
                ).start()
                return carry

            lax.fori_loop(1, count, turn, 0)

        @pl.when(me < count - 1)
        def _():
            deliver(pl.ds(0, 2 * FRAMES), half, pl.ds(FRAMES * me, 2 * FRAMES))

        @pl.when(me == count - 1)
        def _():
            deliver(pl.ds(0, FRAMES), 1, pl.ds(FRAMES * (count - 1), FRAMES))
            deliver(pl.ds(FRAMES, FRAMES), 1, pl.ds(0, FRAMES))

    for position in range(STEPS):
        load(False, position).wait()
        for copy in near(position):
            copy.wait_recv()
        filter_position(position)
        if position == 0:
            constants[0].wait()
        for parity in range(2):
            transform(position, parity)
            for part, (first, positions, channel, channels) in enumerate(PARTS):
                if first + positions - 1 == position and channel + channels - 1 == parity:
                    send_part(part)
    constants[1].wait()

    span = min(256, depth)

    def across(part):
        at, channels = extent(part)
        return pltpu.make_async_remote_copy(
            recv.at[at, :, channels], other.at[at, :, channels], core_send.at[part], core_recv.at[part],
            device_id={"tm": 1 - core}, device_id_type=MESH,
        )

    def turn_part(part, source, base):
        first, positions, channel, channels = PARTS[part]

        def turn_block(position, side):
            def one(parity, carry):
                for piece in range(depth // span):
                    flat = source[position, side, parity, piece * span : (piece + 1) * span, :].T
                    to = slice(base + piece * span, base + (piece + 1) * span)
                    left[side * STEPS + position, parity, 0:TILE, to] = flat
                    left[side * STEPS + position, parity, TILE : 2 * TILE, to] = jnp.dot(
                        flat, whole(turn_ref), preferred_element_type=F32
                    ).astype(BF16)
                return carry

            lax.fori_loop(channel, channel + channels, one, 0)

        for position in range(first, first + positions):
            for side in range(2):
                block = BLOCKS[side][position]
                if block == 2:
                    turn_block(position, side)
                else:
                    pl.when(core == (0 if block < 2 else 1))(functools.partial(turn_block, position, side))

    def multiply_part(part, source, base):
        first, positions, channel, channels = PARTS[part]
        total, codes = codes_of(part)

        def one_unit(step, carry):
            a, b, c = (lax.rem(code, 8) for code in carry[:3])
            slots = [lax.rem(code, 32) for code in carry[3:]]
            for parity in range(channel, channel + channels):
                right = jnp.concatenate(
                    [source[lax.rem(at, STEPS), at // STEPS, parity] for at in (b, c)], 1
                )
                sums = jnp.dot(left[a, parity, :, base : base + depth], right, preferred_element_type=F32)
                parts = []
                for index, slot in enumerate(slots):
                    weight = mask_ref[parity, slot + 18 * core].astype(F32) * scale
                    one = sums[:, index * TILE : (index + 1) * TILE].reshape(2, TILE, TILE) * weight
                    parts.append(one + out_ref[slot, parity] if base else one)
                for slot, one in zip(slots, parts):
                    out_ref[slot, parity] = one
            return tuple(code // 8 for code in carry[:3]) + tuple(code // 32 for code in carry[3:])

        start = tuple(low + core * (high - low) for low, high in zip(*codes))
        lax.fori_loop(0, total, one_unit, start, unroll=total if channels == 1 else 1)

    for part in range(len(PARTS)):
        at, channels = extent(part)
        arrived = recv.at[at, :, channels]
        pltpu.make_async_copy(arrived, arrived, recv_sem.at[part]).wait()
        across(part).start()
        turn_part(part, recv_rows, 0)
        multiply_part(part, recv_rows, 0)
        across(part).wait_recv()
        turn_part(part, other_rows, depth)
        multiply_part(part, other_rows, depth)

    for part in range(len(PARTS)):
        at, channels = extent(part)
        sent = send.at[at, channels, :, pl.ds(0, count - 1)]
        pltpu.make_async_copy(sent, sent, send_sem.at[part]).wait()
        across(part).wait_send()
    for position in range(STEPS):
        for copy in near(position):
            copy.wait_send()


def per_device(count, voltages, filter_taps, block_mask):
    fine = 2 * count
    frames = voltages.reshape(FRAMES, fine, 2, NBLK * TILE)
    depth = 2 * FRAMES * count
    span = min(256, depth)
    table, rotation = dft_table(fine), turn_table(span)
    dma = pltpu.SemaphoreType.DMA
    vmem = pl.BlockSpec(memory_space=pltpu.VMEM)
    anywhere = pl.BlockSpec(memory_space=pl.ANY)
    parts = len(PARTS)
    return pl.pallas_call(
        functools.partial(kernel, count),
        out_shape=pltpu.VMEM((18, 2, 2, TILE, TILE), F32),
        in_specs=[anywhere, vmem, anywhere, anywhere, pl.BlockSpec(memory_space=pltpu.SMEM)],
        out_specs=vmem,
        scratch_shapes=[
            pltpu.VMEM((NBLK, FRAMES, fine, 2, TILE), BF16),
            pltpu.VMEM((STEPS, FRAMES, fine, 2, TILE), BF16),
            pltpu.VMEM((STEPS, FRAMES, fine, 2, TILE), BF16),
            pltpu.VMEM((TAPS, 2 * fine, TILE), F32),
            pltpu.VMEM(table.shape, BF16),
            pltpu.VMEM(rotation.shape, BF16),
            pltpu.VMEM((2 * fine, 2 * FRAMES * TILE), BF16),
            pltpu.VMEM((STEPS, 2, 2 * FRAMES, count, 2, TILE), BF16),
            pltpu.VMEM((STEPS, 2, 2, FRAMES * count, 2, TILE), BF16),
            pltpu.VMEM((STEPS, 2, 2, FRAMES * count, 2, TILE), BF16),
            pltpu.VMEM((NBLK, 2, 2 * TILE, 2 * depth), BF16),
            dma((NBLK,)), dma((2,)), dma((STEPS, 2)), dma((STEPS, 2)), dma((parts,)), dma((parts,)),
            dma((parts,)), dma((parts,)),
        ],
        compiler_params=pltpu.CompilerParams(
            collective_id=0, has_side_effects=True, vmem_limit_bytes=50 * 2**20
        ),
        cost_estimate=pl.CostEstimate(flops=6 * 10**9, bytes_accessed=10**7, transcendentals=0),
        name="correlate",
    )(frames, filter_taps, table, rotation, block_mask.T)


def solution(mesh):
    in_specs = (P("tm", "chan", None, None, None, None), P(), P(None, "chan"))
    out_specs = P("tm", "chan", None, None, None)
    return jax.shard_map(
        functools.partial(per_device, mesh.shape["chan"]),
        mesh=mesh, in_specs=in_specs, out_specs=out_specs, check_vma=False,
    )
```

time: 142 us -> 125 us (0.88)
  Pallas kernels: 131 us -> 121 us
  local copies, waits for them, and re-layouts: 8.49 us -> 2.19 us
    pallas_call x1, Pallas kernels: 131 us -> 121 us  [per_device(): pl.pallas_call(functools.partial(kernel, count), out_shape=pltpu.VMEM((18...]
    unnamed x6 -> x1, local copies, waits for them, and re-layouts: 7.85 us -> 2.19 us
where the time goes in v2:
time: 125 us; the launch traced here: 123 us
  Pallas kernels  121 us (97%)
  local copies, waits for them, and re-layouts  2.19 us (2%)
    pallas_call x1, Pallas kernels, per_device(): pl.pallas_call(functools.partial(kernel, count), out_shape=pltpu.VMEM((18...  121 us

profile of v2, /device:TPU:65, one launch (start us, length us, event | category | flops | bytes accessed | tf_op | source)
XLA Modules:
  0.0 123.0 jit_solution(526527397736821872)
XLA Ops:
  0.0 120.8 %correlate.1 = f32[18,2,2,128,128]{4,3,2,1,0:T(8,128)S(1)} custom-call(bf16[3,256,2,1024]{3,2,1,0:T(2,128)(2,1)} %bitcast.2, f32[4,256]{1,0:T(4,128)} %taps_ref.1, bf16[2,4,128,2,128]{4,3,2,1,0:T(2,128)(2,1)} %constant.4.clone.table_hbm, bf16[2,128,2,128]{3,2,1,0:T(2,128)(2,1)} %constant.5.clone.turn_hbm, s32[2,36]{1,0:T(2,128)} %bitcast.3), custom_call_target="tpu_custom_call" | custom-call | flops 6000000000 | bytes 10000000 | tf_op jit(solution)/shard_map/correlate/pallas_call | solution.py:353
  120.8 2.2 %copy.7 = f32[18,2,2,128,128]{4,3,2,1,0:T(8,128)} copy(f32[18,2,2,128,128]{4,3,2,1,0:T(8,128)S(1)} %correlate.1) | data formatting | bytes 9437184

commit v3 on v2

--- a/solution.py
+++ b/solution.py
@@ -14,6 +14,8 @@
 TILE = 128
 NBLK = 8
 STEPS = 4
+RING = 8
+REACH = 4
 MESH = pl.DeviceIdType.MESH
 BF16 = jnp.bfloat16
 F32 = jnp.float32
@@ -39,8 +41,9 @@
     sine = np.sin(angle) / np.float32(math.sqrt(size))
     upper = np.stack([cosine, sine], 2)
     lower = np.stack([-sine, cosine], 2)
-    table = np.stack([upper, lower], 1).reshape(size // 2, 2, 2, 2 * size)
-    table = np.transpose(table, (1, 0, 2, 3)).reshape(2, size, 2 * size)
+    plane = size // 2 // RING
+    table = np.stack([upper, lower], 1).reshape(plane, RING, 2, 2, 2 * size)
+    table = np.transpose(table, (1, 2, 0, 3, 4)).reshape(RING, 2, 2 * plane, 2 * size)
     return in_tiles(table)
 
 
@@ -104,7 +107,7 @@
 def kernel(
     count,
     v_ref, taps_ref, table_hbm, turn_hbm, mask_ref, out_ref,
-    own, before, after, taps_wide, table_ref, turn_ref, weighted, send, recv, other, left,
+    own, taps_wide, table_ref, turn_ref, weighted, part_send, part_recv, send, recv, other, left,
     load_sem, const_sem, near_send, near_recv, send_sem, recv_sem, core_send, core_recv,
 ):
     me = lax.axis_index("chan")
@@ -112,48 +115,53 @@
     fine = 2 * count
     rows = 2 * fine
     depth = 2 * FRAMES * count
-    half = lax.rem(me, 2)
+    plane = count // RING
+    near_rows = 2 * REACH * plane
+    here = lax.rem(me, RING)
+    column = me // RING
     up = lax.rem(me + 1, count)
     down = lax.rem(me + count - 1, count)
     scale = 1.0 / math.sqrt(FRAMES * count * 2)
 
-    own_rows, before_rows, after_rows = merged(own), merged(before), merged(after)
+    own_rows, table_rows = merged(own), merged(table_ref)
+    part_send_rows, part_recv_rows = merged(part_send), merged(part_recv)
     send_rows, recv_rows, other_rows = merged(send), merged(recv), merged(other)
 
-    def place(away, position):
-        side = 1 - half if away else half
-        return side * STEPS + position
-
-    def load(away, position):
-        index = place(away, position)
-        side = 1 - half if away else half
-        block = BLOCKS[0][position] + side * (BLOCKS[1][position] - BLOCKS[0][position])
-        lanes = pl.ds(pl.multiple_of(block * TILE, TILE), TILE)
+    def load(position, side):
+        block = BLOCKS[side][position]
+        index = side * STEPS + position
+        lanes = pl.ds(block * TILE, TILE)
         return pltpu.make_async_copy(v_ref.at[:, :, :, lanes], own.at[index], load_sem.at[index])
 
-    constants = (
-        pltpu.make_async_copy(table_hbm, table_ref, const_sem.at[0]),
-        pltpu.make_async_copy(turn_hbm, turn_ref, const_sem.at[1]),
-    )
-    for away in (True, False):
-        for position in range(STEPS):
-            load(away, position).start()
-    for copy in constants:
-        copy.start()
+    for position in range(STEPS):
+        for side in range(2):
+            load(position, side).start()
+    for entry in range(RING + 1):
+        pltpu.make_async_copy(
+            table_hbm.at[lax.rem(here + entry + RING - REACH, RING)],
+            table_ref.at[:, :, pl.ds(entry * plane, plane)], const_sem.at[0],
+        ).start()
+    turn_copy = pltpu.make_async_copy(turn_hbm, turn_ref, const_sem.at[1])
+    turn_copy.start()
+
+    def chip(along, across):
+        return lax.rem(column + across, plane) * RING + lax.rem(here + along + RING, RING)
 
     barrier = pltpu.get_barrier_semaphore()
 
-    def greet(offset, carry):
-        peer = lax.rem(me + offset, count)
+    def greet(index, carry):
+        along = index // plane
+        peer = chip(along + along // REACH, lax.rem(index, plane))
         pl.semaphore_signal(barrier, inc=1, device_id={"chan": peer}, device_id_type=MESH)
         return carry
 
-    lax.fori_loop(1, count, greet, 0)
+    greeted = (RING - 1) * plane
+    lax.fori_loop(1, greeted, greet, 0)
     pl.semaphore_signal(barrier, inc=1, device_id={"tm": 1 - core}, device_id_type=MESH)
 
     row = lax.broadcasted_iota(jnp.int32, (rows, fine), 0)
-    column = lax.broadcasted_iota(jnp.int32, (rows, fine), 1)
-    spread = (row // 2 == column).astype(F32)
+    sample = lax.broadcasted_iota(jnp.int32, (rows, fine), 1)
+    spread = (row // 2 == sample).astype(F32)
     for p in range(TAPS):
         wide = jnp.broadcast_to(taps_ref[p : p + 1, :], (TILE, fine))
         taps_wide[p] = lax.dot_general(
@@ -161,59 +169,76 @@
             precision=lax.Precision.HIGHEST, preferred_element_type=F32,
         )
 
-    pl.semaphore_wait(barrier, count)
+    keep = jnp.where(me == count - 1, 0.0, 1.0).astype(F32)
+    group = 16
+    width = 2 * FRAMES * TILE
+
+    def filter_position(position):
+        def filter_rows(step, carry):
+            at = pl.ds(pl.multiple_of(step * group, group), group)
+            taps = [taps_wide[p, at, :] for p in range(TAPS)]
+            for side in range(2):
+                series = [own_rows[side * STEPS + position, f, at, :].astype(F32) for f in range(FRAMES)]
+                for f in range(FRAMES):
+                    mine = taps[0] * series[f]
+                    for p in range(1, f + 1):
+                        mine = mine + taps[p] * series[f - p]
+                    later = taps[f + 1] * series[FRAMES - 1]
+                    for p in range(f + 2, TAPS):
+                        later = later + taps[p] * series[FRAMES + f - p]
+                    to = (side * FRAMES + f) * TILE
+                    weighted[position, at, to : to + TILE] = mine.astype(BF16)
+                    weighted[position, at, width + to : width + to + TILE] = (later * keep).astype(BF16)
+            return carry
+
+        lax.fori_loop(0, rows // group, filter_rows, 0)
+
+    def transform(position, kind, entry, target, added=None):
+        rows_at = slice(2 * plane * entry, 2 * plane * entry + near_rows)
+        tiles = table_rows.shape[1]
+        table = jnp.concatenate(
+            [
+                jnp.concatenate([table_rows[parity, tile, rows_at, :] for tile in range(tiles)], 1)
+                for parity in range(2)
+            ], 0,
+        )
+        for pair in range(FRAMES):
+            base = kind * width + 2 * pair * TILE
+            sums = jnp.dot(table, weighted[position, :, base : base + 2 * TILE], preferred_element_type=F32)
+            for half in range(2):
+                side, f = divmod(2 * pair + half, FRAMES)
+                for parity in range(2):
+                    one = sums[parity * near_rows : (parity + 1) * near_rows, half * TILE : (half + 1) * TILE]
+                    if added is not None:
+                        one = one + added[position, 1 - kind, side, parity, f].astype(F32)
+                    target[position, kind, side, parity, f] = one.astype(BF16)
 
     def near(position):
-        source = own.at[place(True, position)]
         return [
             pltpu.make_async_remote_copy(
-                source, target.at[position], near_send.at[position, way], near_recv.at[position, way],
+                part_send.at[position, kind], part_recv.at[position, kind],
+                near_send.at[position, kind], near_recv.at[position, kind],
                 device_id={"chan": peer}, device_id_type=MESH,
             )
-            for way, (target, peer) in enumerate(((before, up), (after, down)))
+            for kind, peer in enumerate((down, up))
         ]
 
+    def prepare(position):
+        for side in range(2):
+            load(position, side).wait()
+        filter_position(position)
+        if position == 0:
+            pltpu.make_async_copy(table_ref, table_ref, const_sem.at[0]).wait()
+        transform(position, 0, 0, part_send_rows)
+        transform(position, 1, REACH + 1, part_send_rows)
+
+    prepare(0)
+    pl.semaphore_wait(barrier, greeted)
     for position in range(STEPS):
-        load(True, position).wait()
+        if position:
+            prepare(position)
         for copy in near(position):
             copy.start()
-
-    keep_before = jnp.where(me == 0, 0.0, 1.0).astype(F32)
-    keep_own = jnp.where(me == count - 1, 0.0, 1.0).astype(F32)
-    group = 16
-
-    def filter_position(position):
-        index = place(False, position)
-
-        def filter_rows(step, carry):
-            at = pl.ds(pl.multiple_of(step * group, group), group)
-            series = [before_rows[position, f, at, :].astype(F32) for f in range(FRAMES)]
-            series += [own_rows[index, f, at, :].astype(F32) for f in range(FRAMES)]
-            series += [after_rows[position, f, at, :].astype(F32) for f in range(FRAMES)]
-            taps = [taps_wide[p, at, :] for p in range(TAPS)]
-            for f in range(2 * FRAMES):
-                inside = f % FRAMES
-                total = taps[0] * series[FRAMES + f]
-                for p in range(1, inside + 1):
-                    total = total + taps[p] * series[FRAMES + f - p]
-                past = taps[inside + 1] * series[FRAMES + f - inside - 1]
-                for p in range(inside + 2, TAPS):
-                    past = past + taps[p] * series[FRAMES + f - p]
-                total = total + past * (keep_before if f < FRAMES else keep_own)
-                weighted[at, f * TILE : (f + 1) * TILE] = total.astype(BF16)
-            return carry
-
-        lax.fori_loop(0, rows // group, filter_rows, 0)
-
-    def transform(position, parity):
-        table = whole(table_ref, parity)
-        for pair in range(FRAMES):
-            part = jnp.dot(
-                table, weighted[:, pair * 2 * TILE : (pair + 1) * 2 * TILE],
-                preferred_element_type=F32,
-            ).astype(BF16)
-            send_rows[position, parity, 2 * pair] = part[:, :TILE]
-            send_rows[position, parity, 2 * pair + 1] = part[:, TILE:]
 
     def extent(part):
         first, positions, channel, channels = PARTS[part]
@@ -221,46 +246,37 @@
 
     def send_part(part):
         at, channels = extent(part)
-
-        def deliver(source_frames, side, frames):
-            target = recv.at[at, side, channels, frames]
-            pltpu.make_async_copy(
-                send.at[at, channels, source_frames, me], target, recv_sem.at[part]
-            ).start()
-
-            def turn(offset, carry):
-                peer = lax.rem(me + offset, count)
+        targets = [
+            recv.at[at, :, channels, pl.ds(FRAMES * block, FRAMES)] for block in (me, up)
+        ]
+
+        def source(kind, away, across):
+            entry = away if kind == 0 else REACH - 1 - away
+            return send.at[at, kind, :, channels, :, entry * plane + lax.rem(column + across, plane)]
+
+        for kind in range(2):
+            pltpu.make_async_copy(source(kind, 0, 0), targets[kind], recv_sem.at[part]).start()
+
+        def turn(index, carry):
+            away, across = index // plane, lax.rem(index, plane)
+            for kind, way in ((0, 1), (1, -1)):
                 pltpu.make_async_remote_copy(
-                    send.at[at, channels, source_frames, peer], target,
-                    send_sem.at[part], recv_sem.at[part],
-                    device_id={"chan": peer}, device_id_type=MESH,
+                    source(kind, away, across), targets[kind], send_sem.at[part], recv_sem.at[part],
+                    device_id={"chan": chip(way * away, across)}, device_id_type=MESH,
                 ).start()
-                return carry
-
-            lax.fori_loop(1, count, turn, 0)
-
-        @pl.when(me < count - 1)
-        def _():
-            deliver(pl.ds(0, 2 * FRAMES), half, pl.ds(FRAMES * me, 2 * FRAMES))
-
-        @pl.when(me == count - 1)
-        def _():
-            deliver(pl.ds(0, FRAMES), 1, pl.ds(FRAMES * (count - 1), FRAMES))
-            deliver(pl.ds(FRAMES, FRAMES), 1, pl.ds(0, FRAMES))
+            return carry
+
+        lax.fori_loop(1, REACH * plane, turn, 0)
 
     for position in range(STEPS):
-        load(False, position).wait()
         for copy in near(position):
             copy.wait_recv()
-        filter_position(position)
-        if position == 0:
-            constants[0].wait()
-        for parity in range(2):
-            transform(position, parity)
-            for part, (first, positions, channel, channels) in enumerate(PARTS):
-                if first + positions - 1 == position and channel + channels - 1 == parity:
-                    send_part(part)
-    constants[1].wait()
+        transform(position, 0, REACH, send_rows, part_recv_rows)
+        transform(position, 1, 1, send_rows, part_recv_rows)
+        for part, (first, positions, _, _) in enumerate(PARTS):
+            if first + positions - 1 == position:
+                send_part(part)
+    turn_copy.wait()
 
     span = min(256, depth)
 
@@ -332,7 +348,7 @@
 
     for part in range(len(PARTS)):
         at, channels = extent(part)
-        sent = send.at[at, channels, :, pl.ds(0, count - 1)]
+        sent = send.at[at, :, :, channels, :, pl.ds(0, REACH * plane - 1)]
         pltpu.make_async_copy(sent, sent, send_sem.at[part]).wait()
         across(part).wait_send()
     for position in range(STEPS):
@@ -350,6 +366,7 @@
     vmem = pl.BlockSpec(memory_space=pltpu.VMEM)
     anywhere = pl.BlockSpec(memory_space=pl.ANY)
     parts = len(PARTS)
+    spectra = (STEPS, 2, 2, 2, FRAMES, REACH * (count // RING), 2, TILE)
     return pl.pallas_call(
         functools.partial(kernel, count),
         out_shape=pltpu.VMEM((18, 2, 2, TILE, TILE), F32),
@@ -357,13 +374,13 @@
         out_specs=vmem,
         scratch_shapes=[
             pltpu.VMEM((NBLK, FRAMES, fine, 2, TILE), BF16),
-            pltpu.VMEM((STEPS, FRAMES, fine, 2, TILE), BF16),
-            pltpu.VMEM((STEPS, FRAMES, fine, 2, TILE), BF16),
             pltpu.VMEM((TAPS, 2 * fine, TILE), F32),
-            pltpu.VMEM(table.shape, BF16),
+            pltpu.VMEM(table.shape[1:3] + ((RING + 1) * (count // RING),) + table.shape[4:], BF16),
             pltpu.VMEM(rotation.shape, BF16),
-            pltpu.VMEM((2 * fine, 2 * FRAMES * TILE), BF16),
-            pltpu.VMEM((STEPS, 2, 2 * FRAMES, count, 2, TILE), BF16),
+            pltpu.VMEM((STEPS, 2 * fine, 4 * FRAMES * TILE), BF16),
+            pltpu.VMEM(spectra, BF16),
+            pltpu.VMEM(spectra, BF16),
+            pltpu.VMEM(spectra, BF16),
             pltpu.VMEM((STEPS, 2, 2, FRAMES * count, 2, TILE), BF16),
             pltpu.VMEM((STEPS, 2, 2, FRAMES * count, 2, TILE), BF16),
             pltpu.VMEM((NBLK, 2, 2 * TILE, 2 * depth), BF16),
@@ -371,7 +388,7 @@
             dma((parts,)), dma((parts,)),
         ],
         compiler_params=pltpu.CompilerParams(
-            collective_id=0, has_side_effects=True, vmem_limit_bytes=50 * 2**20
+            collective_id=0, has_side_effects=True, vmem_limit_bytes=54 * 2**20
         ),
         cost_estimate=pl.CostEstimate(flops=6 * 10**9, bytes_accessed=10**7, transcendentals=0),
         name="correlate",

time: 125 us -> 111 us (0.89); the launches traced: 123 us -> 111 us
  Pallas kernels: 121 us -> 109 us
    pallas_call x1, Pallas kernels: 121 us -> 109 us  [per_device(): pl.pallas_call(functools.partial(kernel, count), out_shape=pltpu.VMEM((18...]
where the time goes in v3:
time: 111 us
  Pallas kernels  109 us (98%)
  local copies, waits for them, and re-layouts  2.19 us (2%)
    pallas_call x1, Pallas kernels, per_device(): pl.pallas_call(functools.partial(kernel, count), out_shape=pltpu.VMEM((18...  109 us

profile of v3, /device:TPU:65, one launch (start us, length us, event | category | flops | bytes accessed | tf_op | source)
XLA Modules:
  0.0 110.7 jit_solution(1199200699676703509)
XLA Ops:
  0.0 108.5 %correlate.1 = f32[18,2,2,128,128]{4,3,2,1,0:T(8,128)S(1)} custom-call(bf16[3,256,2,1024]{3,2,1,0:T(2,128)(2,1)} %bitcast.2, f32[4,256]{1,0:T(4,128)} %taps_ref.1, bf16[8,2,4,16,2,128]{5,4,3,2,1,0:T(2,128)(2,1)} %constant.4.clone.table_hbm, bf16[2,128,2,128]{3,2,1,0:T(2,128)(2,1)} %constant.5.clone.turn_hbm, s32[2,36]{1,0:T(2,128)} %bitcast.3), custom_call_target="tpu_custom_call" | custom-call | flops 6000000000 | bytes 10000000 | tf_op jit(solution)/shard_map/correlate/pallas_call | solution.py:370
  108.5 2.2 %copy.7 = f32[18,2,2,128,128]{4,3,2,1,0:T(8,128)} copy(f32[18,2,2,128,128]{4,3,2,1,0:T(8,128)S(1)} %correlate.1) | data formatting | bytes 9437184

commit v4 on v3

--- a/solution.py
+++ b/solution.py
@@ -56,7 +56,12 @@
 
 
 BLOCKS = ((0, 1, 3, 2), (5, 6, 7, 4))
-PARTS = ((0, 1, 0, 2), (1, 2, 0, 2), (3, 1, 0, 1), (3, 1, 1, 1))
+PARTS = ((0, 1, 0, 2, 0, 2), (1, 2, 0, 2, 0, 2), (3, 1, 0, 1, 0, 2), (3, 1, 1, 1, 0, 1), (3, 1, 1, 1, 1, 1))
+
+
+def places_in(part):
+    first, positions, side, sides = PARTS[part][:4]
+    return {s * STEPS + p for s in range(side, side + sides) for p in range(first, first + positions)}
 
 
 def place_of(block):
@@ -65,16 +70,15 @@
 
 
 def units_of(part, core):
-    first, positions = PARTS[part][:2]
-    ready = range(first + positions)
-    fresh = range(first, first + positions)
+    fresh = places_in(part)
+    ready = set().union(*(places_in(earlier) for earlier in range(part + 1)))
     units = []
     for a in range(NBLK):
         row = []
         for b in range(a, NBLK):
             slot = PAIRS.index((a, b)) - 18 * core
-            at = (place_of(a) % STEPS, place_of(b) % STEPS)
-            if 0 <= slot < 18 and max(at) in fresh and max(at) in ready:
+            at = {place_of(a), place_of(b)}
+            if 0 <= slot < 18 and at & fresh and at <= ready:
                 row.append((b, slot))
         if len(row) % 2:
             row.append(row[-1])
@@ -108,7 +112,7 @@
     count,
     v_ref, taps_ref, table_hbm, turn_hbm, mask_ref, out_ref,
     own, taps_wide, table_ref, turn_ref, weighted, part_send, part_recv, send, recv, other, left,
-    load_sem, const_sem, near_send, near_recv, send_sem, recv_sem, core_send, core_recv,
+    load_sem, const_sem, near_send, near_recv, send_sem, recv_sem, core_send, core_recv, met_sem,
 ):
     me = lax.axis_index("chan")
     core = lax.axis_index("tm")
@@ -149,15 +153,27 @@
 
     barrier = pltpu.get_barrier_semaphore()
 
-    def greet(index, carry):
-        along = index // plane
-        peer = chip(along + along // REACH, lax.rem(index, plane))
+    def tell_group(semaphore):
+        def tell(along, across):
+            peer = chip(along, across)
+            pl.semaphore_signal(semaphore, inc=1, device_id={"chan": peer}, device_id_type=MESH)
+
+        def tell_ring(index, carry):
+            tell(index, 0)
+            return carry
+
+        def tell_plane(index, carry):
+            tell(0, index)
+            return carry
+
+        lax.fori_loop(1, RING, tell_ring, 0)
+        lax.fori_loop(1, plane, tell_plane, 0)
+
+    group_size = RING - 1 + plane - 1
+    for peer in (up, down):
         pl.semaphore_signal(barrier, inc=1, device_id={"chan": peer}, device_id_type=MESH)
-        return carry
-
-    greeted = (RING - 1) * plane
-    lax.fori_loop(1, greeted, greet, 0)
     pl.semaphore_signal(barrier, inc=1, device_id={"tm": 1 - core}, device_id_type=MESH)
+    tell_group(barrier)
 
     row = lax.broadcasted_iota(jnp.int32, (rows, fine), 0)
     sample = lax.broadcasted_iota(jnp.int32, (rows, fine), 1)
@@ -233,26 +249,28 @@
         transform(position, 1, REACH + 1, part_send_rows)
 
     prepare(0)
-    pl.semaphore_wait(barrier, greeted)
+    pl.semaphore_wait(barrier, group_size + 3)
     for position in range(STEPS):
         if position:
             prepare(position)
         for copy in near(position):
             copy.start()
+        if position == 0:
+            tell_group(met_sem)
 
     def extent(part):
-        first, positions, channel, channels = PARTS[part]
-        return pl.ds(first, positions), pl.ds(channel, channels)
+        first, positions, side, sides, channel, channels = PARTS[part]
+        return pl.ds(first, positions), pl.ds(side, sides), pl.ds(channel, channels)
 
     def send_part(part):
-        at, channels = extent(part)
+        at, sides, channels = extent(part)
         targets = [
-            recv.at[at, :, channels, pl.ds(FRAMES * block, FRAMES)] for block in (me, up)
+            recv.at[at, sides, channels, pl.ds(FRAMES * block, FRAMES)] for block in (me, up)
         ]
 
         def source(kind, away, across):
             entry = away if kind == 0 else REACH - 1 - away
-            return send.at[at, kind, :, channels, :, entry * plane + lax.rem(column + across, plane)]
+            return send.at[at, kind, sides, channels, :, entry * plane + lax.rem(column + across, plane)]
 
         for kind in range(2):
             pltpu.make_async_copy(source(kind, 0, 0), targets[kind], recv_sem.at[part]).start()
@@ -271,24 +289,26 @@
     for position in range(STEPS):
         for copy in near(position):
             copy.wait_recv()
+        if position == 0:
+            pl.semaphore_wait(met_sem, group_size)
         transform(position, 0, REACH, send_rows, part_recv_rows)
         transform(position, 1, 1, send_rows, part_recv_rows)
-        for part, (first, positions, _, _) in enumerate(PARTS):
-            if first + positions - 1 == position:
+        for part in range(len(PARTS)):
+            if PARTS[part][0] + PARTS[part][1] - 1 == position:
                 send_part(part)
     turn_copy.wait()
 
     span = min(256, depth)
 
     def across(part):
-        at, channels = extent(part)
+        at, sides, channels = extent(part)
         return pltpu.make_async_remote_copy(
-            recv.at[at, :, channels], other.at[at, :, channels], core_send.at[part], core_recv.at[part],
+            recv.at[at, sides, channels], other.at[at, sides, channels], core_send.at[part], core_recv.at[part],
             device_id={"tm": 1 - core}, device_id_type=MESH,
         )
 
     def turn_part(part, source, base):
-        first, positions, channel, channels = PARTS[part]
+        first, positions, first_side, sides, channel, channels = PARTS[part]
 
         def turn_block(position, side):
             def one(parity, carry):
@@ -304,7 +324,7 @@
             lax.fori_loop(channel, channel + channels, one, 0)
 
         for position in range(first, first + positions):
-            for side in range(2):
+            for side in range(first_side, first_side + sides):
                 block = BLOCKS[side][position]
                 if block == 2:
                     turn_block(position, side)
@@ -312,7 +332,7 @@
                     pl.when(core == (0 if block < 2 else 1))(functools.partial(turn_block, position, side))
 
     def multiply_part(part, source, base):
-        first, positions, channel, channels = PARTS[part]
+        channel, channels = PARTS[part][4:]
         total, codes = codes_of(part)
 
         def one_unit(step, carry):
@@ -336,8 +356,8 @@
         lax.fori_loop(0, total, one_unit, start, unroll=total if channels == 1 else 1)
 
     for part in range(len(PARTS)):
-        at, channels = extent(part)
-        arrived = recv.at[at, :, channels]
+        at, sides, channels = extent(part)
+        arrived = recv.at[at, sides, channels]
         pltpu.make_async_copy(arrived, arrived, recv_sem.at[part]).wait()
         across(part).start()
         turn_part(part, recv_rows, 0)
@@ -347,8 +367,8 @@
         multiply_part(part, other_rows, depth)
 
     for part in range(len(PARTS)):
-        at, channels = extent(part)
-        sent = send.at[at, :, :, channels, :, pl.ds(0, REACH * plane - 1)]
+        at, sides, channels = extent(part)
+        sent = send.at[at, :, sides, channels, :, pl.ds(0, REACH * plane - 1)]
         pltpu.make_async_copy(sent, sent, send_sem.at[part]).wait()
         across(part).wait_send()
     for position in range(STEPS):
@@ -385,7 +405,7 @@
             pltpu.VMEM((STEPS, 2, 2, FRAMES * count, 2, TILE), BF16),
             pltpu.VMEM((NBLK, 2, 2 * TILE, 2 * depth), BF16),
             dma((NBLK,)), dma((2,)), dma((STEPS, 2)), dma((STEPS, 2)), dma((parts,)), dma((parts,)),
-            dma((parts,)), dma((parts,)),
+            dma((parts,)), dma((parts,)), pltpu.SemaphoreType.REGULAR,
         ],
         compiler_params=pltpu.CompilerParams(
             collective_id=0, has_side_effects=True, vmem_limit_bytes=54 * 2**20

time: 111 us -> 110 us (level)
  no operation moved by 1% of the time
where the time goes in v4:
time: 110 us
  Pallas kernels  108 us (98%)
  local copies, waits for them, and re-layouts  2.19 us (2%)
    pallas_call x1, Pallas kernels, per_device(): pl.pallas_call(functools.partial(kernel, count), out_shape=pltpu.VMEM((18...  108 us

profile of v4, /device:TPU:65, one launch (start us, length us, event | category | flops | bytes accessed | tf_op | source)
XLA Modules:
  0.0 110.3 jit_solution(12081335703412248063)
XLA Ops:
  0.0 108.1 %correlate.1 = f32[18,2,2,128,128]{4,3,2,1,0:T(8,128)S(1)} custom-call(bf16[3,256,2,1024]{3,2,1,0:T(2,128)(2,1)} %bitcast.2, f32[4,256]{1,0:T(4,128)} %taps_ref.1, bf16[8,2,4,16,2,128]{5,4,3,2,1,0:T(2,128)(2,1)} %constant.4.clone.table_hbm, bf16[2,128,2,128]{3,2,1,0:T(2,128)(2,1)} %constant.5.clone.turn_hbm, s32[2,36]{1,0:T(2,128)} %bitcast.3), custom_call_target="tpu_custom_call" | custom-call | flops 6000000000 | bytes 10000000 | tf_op jit(solution)/shard_map/correlate/pallas_call | solution.py:390
  108.1 2.2 %copy.7 = f32[18,2,2,128,128]{4,3,2,1,0:T(8,128)} copy(f32[18,2,2,128,128]{4,3,2,1,0:T(8,128)S(1)} %correlate.1) | data formatting | bytes 9437184

commit v5 on v4

--- a/solution.py
+++ b/solution.py
@@ -43,7 +43,8 @@
     lower = np.stack([-sine, cosine], 2)
     plane = size // 2 // RING
     table = np.stack([upper, lower], 1).reshape(plane, RING, 2, 2, 2 * size)
-    table = np.transpose(table, (1, 2, 0, 3, 4)).reshape(RING, 2, 2 * plane, 2 * size)
+    table = np.transpose(table, (2, 1, 0, 3, 4))
+    table = np.concatenate([table, table], 1).reshape(2, 4 * RING * plane, 2 * size)
     return in_tiles(table)
 
 
@@ -55,8 +56,8 @@
     return in_tiles(turn)
 
 
-BLOCKS = ((0, 1, 3, 2), (5, 6, 7, 4))
-PARTS = ((0, 1, 0, 2, 0, 2), (1, 2, 0, 2, 0, 2), (3, 1, 0, 1, 0, 2), (3, 1, 1, 1, 0, 1), (3, 1, 1, 1, 1, 1))
+BLOCKS = ((0, 3, 1, 2), (5, 7, 6, 4))
+PARTS = ((0, 1, 0, 2, 0, 2), (1, 1, 0, 2, 0, 2), (2, 1, 0, 2, 0, 2), (3, 1, 0, 1, 0, 2), (3, 1, 1, 1, 0, 1), (3, 1, 1, 1, 1, 1))
 
 
 def places_in(part):
@@ -93,14 +94,16 @@
     codes = []
     for mine in units:
         while len(mine) < count:
-            index = next(i for i, unit in enumerate(mine) if unit[3] != unit[4])
+            index = next((i for i, unit in enumerate(mine) if unit[3] != unit[4]), None)
+            if index is None:
+                break
             a, b, c, slot, other = mine[index]
             mine[index : index + 1] = [(a, b, b, slot, slot), (a, c, c, other, other)]
         codes.append([
             sum(unit[field] * base**place for place, unit in enumerate(mine))
             for field, base in enumerate((8, 8, 8, 32, 32))
         ])
-    return count, codes
+    return [len(mine) for mine in units], codes
 
 
 def merged(ref):
@@ -137,16 +140,15 @@
         lanes = pl.ds(block * TILE, TILE)
         return pltpu.make_async_copy(v_ref.at[:, :, :, lanes], own.at[index], load_sem.at[index])
 
-    for position in range(STEPS):
-        for side in range(2):
-            load(position, side).start()
-    for entry in range(RING + 1):
-        pltpu.make_async_copy(
-            table_hbm.at[lax.rem(here + entry + RING - REACH, RING)],
-            table_ref.at[:, :, pl.ds(entry * plane, plane)], const_sem.at[0],
-        ).start()
+    entries = (RING + 1) * plane
+    first_entry = lax.rem(here + RING - REACH, RING) * plane
+    table_copy = pltpu.make_async_copy(
+        table_hbm.at[:, :, pl.ds(first_entry, entries)], table_ref, const_sem.at[0]
+    )
     turn_copy = pltpu.make_async_copy(turn_hbm, turn_ref, const_sem.at[1])
-    turn_copy.start()
+    for side in range(2):
+        load(0, side).start()
+    table_copy.start()
 
     def chip(along, across):
         return lax.rem(column + across, plane) * RING + lax.rem(here + along + RING, RING)
@@ -174,6 +176,10 @@
         pl.semaphore_signal(barrier, inc=1, device_id={"chan": peer}, device_id_type=MESH)
     pl.semaphore_signal(barrier, inc=1, device_id={"tm": 1 - core}, device_id_type=MESH)
     tell_group(barrier)
+    for position in range(1, STEPS):
+        for side in range(2):
+            load(position, side).start()
+    turn_copy.start()
 
     row = lax.broadcasted_iota(jnp.int32, (rows, fine), 0)
     sample = lax.broadcasted_iota(jnp.int32, (rows, fine), 1)
@@ -244,7 +250,7 @@
             load(position, side).wait()
         filter_position(position)
         if position == 0:
-            pltpu.make_async_copy(table_ref, table_ref, const_sem.at[0]).wait()
+            table_copy.wait()
         transform(position, 0, 0, part_send_rows)
         transform(position, 1, REACH + 1, part_send_rows)
 
@@ -333,7 +339,7 @@
 
     def multiply_part(part, source, base):
         channel, channels = PARTS[part][4:]
-        total, codes = codes_of(part)
+        (total, other_total), codes = codes_of(part)
 
         def one_unit(step, carry):
             a, b, c = (lax.rem(code, 8) for code in carry[:3])
@@ -353,18 +359,26 @@
             return tuple(code // 8 for code in carry[:3]) + tuple(code // 32 for code in carry[3:])
 
         start = tuple(low + core * (high - low) for low, high in zip(*codes))
-        lax.fori_loop(0, total, one_unit, start, unroll=total if channels == 1 else 1)
+        if total == other_total:
+            lax.fori_loop(0, total, one_unit, start, unroll=total if channels == 1 else 1)
+        else:
+            lax.fori_loop(0, total + core * (other_total - total), one_unit, start)
+
+    def finish(part):
+        across(part).wait_recv()
+        turn_part(part, other_rows, depth)
+        multiply_part(part, other_rows, depth)
 
     for part in range(len(PARTS)):
         at, sides, channels = extent(part)
         arrived = recv.at[at, sides, channels]
         pltpu.make_async_copy(arrived, arrived, recv_sem.at[part]).wait()
         across(part).start()
+        if part:
+            finish(part - 1)
         turn_part(part, recv_rows, 0)
         multiply_part(part, recv_rows, 0)
-        across(part).wait_recv()
-        turn_part(part, other_rows, depth)
-        multiply_part(part, other_rows, depth)
+    finish(len(PARTS) - 1)
 
     for part in range(len(PARTS)):
         at, sides, channels = extent(part)
@@ -395,7 +409,7 @@
         scratch_shapes=[
             pltpu.VMEM((NBLK, FRAMES, fine, 2, TILE), BF16),
             pltpu.VMEM((TAPS, 2 * fine, TILE), F32),
-            pltpu.VMEM(table.shape[1:3] + ((RING + 1) * (count // RING),) + table.shape[4:], BF16),
+            pltpu.VMEM(table.shape[:2] + ((RING + 1) * (count // RING),) + table.shape[3:], BF16),
             pltpu.VMEM(rotation.shape, BF16),
             pltpu.VMEM((STEPS, 2 * fine, 4 * FRAMES * TILE), BF16),
             pltpu.VMEM(spectra, BF16),

time: 110 us -> 113 us (1.027)
  Pallas kernels: 108 us -> 110 us
    pallas_call x1, Pallas kernels: 108 us -> 110 us  [per_device(): pl.pallas_call(functools.partial(kernel, count), out_shape=pltpu.VMEM((18...]
where the time goes in v5:
time: 113 us
  Pallas kernels  110 us (97%)
  local copies, waits for them, and re-layouts  2.19 us (2%)
    pallas_call x1, Pallas kernels, per_device(): pl.pallas_call(functools.partial(kernel, count), out_shape=pltpu.VMEM((18...  110 us

profile of v5, /device:TPU:65, one launch (start us, length us, event | category | flops | bytes accessed | tf_op | source)
XLA Modules:
  0.0 112.5 jit_solution(6901810239444620784)
XLA Ops:
  0.0 110.3 %correlate.1 = f32[18,2,2,128,128]{4,3,2,1,0:T(8,128)S(1)} custom-call(bf16[3,256,2,1024]{3,2,1,0:T(2,128)(2,1)} %bitcast.2, f32[4,256]{1,0:T(4,128)} %taps_ref.1, bf16[2,4,256,2,128]{4,3,2,1,0:T(2,128)(2,1)} %constant.4.clone.table_hbm, bf16[2,128,2,128]{3,2,1,0:T(2,128)(2,1)} %constant.5.clone.turn_hbm, s32[2,36]{1,0:T(2,128)} %bitcast.3), custom_call_target="tpu_custom_call" | custom-call | flops 6000000000 | bytes 10000000 | tf_op jit(solution)/shard_map/correlate/pallas_call | solution.py:404
  110.3 2.2 %copy.7 = f32[18,2,2,128,128]{4,3,2,1,0:T(8,128)} copy(f32[18,2,2,128,128]{4,3,2,1,0:T(8,128)S(1)} %correlate.1) | data formatting | bytes 9437184

commit v6 on v5

--- a/solution.py
+++ b/solution.py
@@ -56,8 +56,8 @@
     return in_tiles(turn)
 
 
-BLOCKS = ((0, 3, 1, 2), (5, 7, 6, 4))
-PARTS = ((0, 1, 0, 2, 0, 2), (1, 1, 0, 2, 0, 2), (2, 1, 0, 2, 0, 2), (3, 1, 0, 1, 0, 2), (3, 1, 1, 1, 0, 1), (3, 1, 1, 1, 1, 1))
+BLOCKS = ((0, 1, 3, 2), (5, 6, 7, 4))
+PARTS = ((0, 1, 0, 2, 0, 2), (1, 2, 0, 2, 0, 2), (3, 1, 0, 1, 0, 2), (3, 1, 1, 1, 0, 2))
 
 
 def places_in(part):
@@ -360,7 +360,7 @@
 
         start = tuple(low + core * (high - low) for low, high in zip(*codes))
         if total == other_total:
-            lax.fori_loop(0, total, one_unit, start, unroll=total if channels == 1 else 1)
+            lax.fori_loop(0, total, one_unit, start, unroll=total if total <= 3 else 1)
         else:
             lax.fori_loop(0, total + core * (other_total - total), one_unit, start)
 
@@ -374,11 +374,9 @@
         arrived = recv.at[at, sides, channels]
         pltpu.make_async_copy(arrived, arrived, recv_sem.at[part]).wait()
         across(part).start()
-        if part:
-            finish(part - 1)
         turn_part(part, recv_rows, 0)
         multiply_part(part, recv_rows, 0)
-    finish(len(PARTS) - 1)
+        finish(part)
 
     for part in range(len(PARTS)):
         at, sides, channels = extent(part)

time: 113 us -> 109 us (0.965)
  Pallas kernels: 110 us -> 107 us
    pallas_call x1, Pallas kernels: 110 us -> 107 us  [per_device(): pl.pallas_call(functools.partial(kernel, count), out_shape=pltpu.VMEM((18...]
where the time goes in v6:
time: 109 us
  Pallas kernels  107 us (98%)
  local copies, waits for them, and re-layouts  2.19 us (2%)
    pallas_call x1, Pallas kernels, per_device(): pl.pallas_call(functools.partial(kernel, count), out_shape=pltpu.VMEM((18...  107 us
    unnamed x1, local copies, waits for them, and re-layouts  2.19 us

profile of v6, /device:TPU:65, one launch (start us, length us, event | category | flops | bytes accessed | tf_op | source)
XLA Modules:
  0.0 108.7 jit_solution(14196676025476423186)
XLA Ops:
  0.0 106.5 %correlate.1 = f32[18,2,2,128,128]{4,3,2,1,0:T(8,128)S(1)} custom-call(bf16[3,256,2,1024]{3,2,1,0:T(2,128)(2,1)} %bitcast.2, f32[4,256]{1,0:T(4,128)} %taps_ref.1, bf16[2,4,256,2,128]{4,3,2,1,0:T(2,128)(2,1)} %constant.4.clone.table_hbm, bf16[2,128,2,128]{3,2,1,0:T(2,128)(2,1)} %constant.5.clone.turn_hbm, s32[2,36]{1,0:T(2,128)} %bitcast.3), custom_call_target="tpu_custom_call" | custom-call | flops 6000000000 | bytes 10000000 | tf_op jit(solution)/shard_map/correlate/pallas_call | solution.py:402
  106.6 2.2 %copy.7 = f32[18,2,2,128,128]{4,3,2,1,0:T(8,128)} copy(f32[18,2,2,128,128]{4,3,2,1,0:T(8,128)S(1)} %correlate.1) | data formatting | bytes 9437184
